TPU v7x, 32 devices: a whole 2x2x4 slice. The times are simulated.
32 devices in a mesh: grp: 2 (over x), gy: 8 (over z, y), ch: 2 (over core).
Axes of the slice: x: 2, y: 2, z: 4, core: 2. Of those that a mesh axis runs over, the one named last changes fastest.
Arguments:
- inputs: bfloat16 [256, 8, 16, 256], P(None, 'gy', 'grp'), parts along dimension 2, may hold values from -6 to 6
- cotangent: bfloat16 [256, 8, 16, 256], P('ch', 'gy', 'grp'), parts along dimension 2, may hold values from -6 to 6
- weight: bfloat16 [27, 256, 256], P(None, None, 'ch'), may hold values from -0.078125 to 0.078125
Outputs:
- input_grad: bfloat16 [256, 8, 16, 256], P('ch', 'gy', 'grp'), parts along dimension 2
- weight_grad: float32 [54, 256, 256], P('grp', None, 'ch'), parts along dimension 0
There are 2 independent parts, one for each index of `grp`. A program takes and returns all parts, laid end to end along the dimension named above; an argument that names none is the same for every part. Nothing has to cross between parts.
All inputs are finite; a program needn't handle non-finite values.
Results may differ from a plain program's by a relative error of at most 0.0013.
Values may be sent and summed in bfloat16 or wider, within the bound.
A program may use at most 192 MiB of HBM per device.

v0:
```python
import math

import jax
import jax.numpy as jnp
from jax import lax
from jax.sharding import PartitionSpec as P


def padded(block, sides, width):
    for axis, dim in sides:
        count = lax.axis_size(axis)
        forward = [(i, i + 1) for i in range(count - 1)]
        backward = [(target, source) for source, target in forward]
        low = lax.ppermute(
            lax.slice_in_dim(block, block.shape[dim] - width, None, axis=dim), axis, forward
        )
        high = lax.ppermute(lax.slice_in_dim(block, 0, width, axis=dim), axis, backward)
        block = jnp.concatenate([low, block, high], axis=dim)
    return block


def shift_cells(flat, z_step, x_step, x_count):
    offset = z_step * x_count + x_step
    length = flat.shape[-1]
    if offset > 0:
        filler = jnp.zeros(flat.shape[:-1] + (offset,), flat.dtype)
        moved = jnp.concatenate([filler, flat[..., : length - offset]], axis=-1)
    elif offset < 0:
        filler = jnp.zeros(flat.shape[:-1] + (-offset,), flat.dtype)
        moved = jnp.concatenate([flat[..., -offset:], filler], axis=-1)
    else:
        moved = flat
    if x_step == 0:
        return moved
    column = jnp.arange(length) % x_count - x_step
    keep = (column >= 0) & (column < x_count)
    return jnp.where(keep, moved, jnp.zeros((), flat.dtype))


def grad_group(planes, y_off, x_count):
    row_count = planes.shape[1] - 2
    flat = planes.reshape(planes.shape[0], planes.shape[1], -1)
    window = flat[:, 2 - y_off : 2 - y_off + row_count, :]
    pieces_list = []
    for z_off in range(3):
        for x_off in range(3):
            pieces_list.append(shift_cells(window, z_off - 1, x_off - 1, x_count))
    stacked = jnp.stack(pieces_list, 0)
    return stacked.reshape(9 * planes.shape[0], -1)


def local(inputs, cotangent, weight):
    channel_count = inputs.shape[0]
    local_out = cotangent.shape[0]
    row_count = inputs.shape[1]
    z_count = inputs.shape[2]
    x_count = inputs.shape[3]
    cell_count = row_count * z_count * x_count
    owned_rows = channel_count // lax.axis_size("ch")
    weight_rows = jnp.transpose(weight, (1, 0, 2))
    planes = padded(cotangent, (("gy", 1),), 1)
    stacks = []
    stacks = [grad_group(planes, y_off, x_count) for y_off in range(3)]
    summed = jnp.zeros((owned_rows * lax.axis_size("ch"), cell_count), jnp.float32)
    for partial_y_off in range(3):
        tap_cols = weight_rows[:, 9 * partial_y_off : 9 * partial_y_off + 9, :].reshape(
            owned_rows * lax.axis_size("ch"), -1
        )
        summed = summed + jnp.dot(
            tap_cols, stacks[partial_y_off], preferred_element_type=jnp.float32
        )
    grad_rows = lax.psum_scatter(summed, "ch", scatter_dimension=0, tiled=True)
    input_grad = grad_rows.astype(jnp.bfloat16).reshape(owned_rows, row_count, z_count, x_count)
    tap_grads = []
    input_halo = padded(inputs, (("gy", 1),), 1)
    halo_flat = input_halo.reshape(channel_count, row_count + 2, -1)
    grad_flat = cotangent.reshape(local_out, -1)
    for y_off in range(3):
        window = halo_flat[:, y_off : y_off + row_count, :]
        for z_off in range(3):
            for x_off in range(3):
                moved = shift_cells(window, 1 - z_off, 1 - x_off, x_count).reshape(
                    channel_count, -1
                )
                tap_grads.append(
                    lax.dot_general(
                        moved,
                        grad_flat,
                        (((1,), (1,)), ((), ())),
                        preferred_element_type=jnp.float32,
                    )
                )
    local_grad = jnp.stack(tap_grads, 0)
    norm_factor = 1.0 / math.sqrt(row_count * lax.axis_size("gy") * z_count * x_count)
    weight_grad = lax.psum(local_grad, "gy") * norm_factor
    return (input_grad, weight_grad)


def solution(mesh):
    placed = (P(None, "gy", "grp", None), P("ch", "gy", "grp", None), P(None, None, "ch"))
    return jax.shard_map(
        local,
        mesh=mesh,
        in_specs=placed,
        out_specs=(P("ch", "gy", "grp", None), P("grp", None, "ch")),
        check_vma=False,
    )
```

profile of v0, /device:TPU:0, one launch (start us, length us, event | category | flops | bytes accessed | tf_op | source)
XLA Modules:
  0.0 311.7 jit_solution(372415313402467962)
XLA Ops:
  8.1 2.3 copy.71
  10.3 1.3 collective-permute-start.1
  11.6 6.3 %collective-permute-start = (bf16[128,1,8,256]{0,3,2,1:T(8,128)(2,1)}, bf16[128,1,8,256]{0,3,2,1:T(8,128)(2,1)}, u32[]{:S(2)}, u32[]{:S(2)}) collective-permute-start(bf16[128,1,8,256]{0,3,2,1:T(8,128)(2,1)} %copy.71), channel_id=1, source_target_pairs={{0,2},{2,4},{4,6},{6,8},{8,10},{10,12},{12,14},{1,3},{3,5},{5,7},{... | collective-permute-start | bytes 1572872 | tf_op jit(solution)/shard_map/ppermute | solution.py:14
  17.9 1.6 copy.80
  19.6 1.3 collective-permute-start.3
  20.9 5.6 %collective-permute-start.2 = (bf16[256,1,8,256]{0,3,2,1:T(8,128)(2,1)S(1)}, bf16[256,1,8,256]{0,3,2,1:T(8,128)(2,1)}, u32[]{:S(2)}, u32[]{:S(2)}) collective-permute-start(bf16[256,1,8,256]{0,3,2,1:T(8,128)(2,1)S(1)} %copy.80), channel_id=1, source_target_pairs={{0,2},{2,4},{4,6},{6,8},{8,10},{10,12},{12,14},{1,3},{3,5},{5,7},{... | collective-permute-start | bytes 3145736 | tf_op jit(solution)/shard_map/ppermute | solution.py:14
  26.5 2.6 copy.75
  30.1 1.2 fusion.160
  31.4 30.0 %collective-permute-done = bf16[128,1,8,256]{0,3,2,1:T(8,128)(2,1)} collective-permute-done((bf16[128,1,8,256]{0,3,2,1:T(8,128)(2,1)}, bf16[128,1,8,256]{0,3,2,1:T(8,128)(2,1)}, u32[]{:S(2)}, u32[]{:S(2)}) %collective-permute-start) | collective-permute-done | bytes 524320 | tf_op jit(solution)/shard_map/ppermute | solution.py:14
  61.4 1.5 pad_maximum_fusion.1
  62.9 1.3 fusion.161
  64.2 1.2 fusion.162
  65.4 1.2 fusion.163
  66.6 1.6 fusion.164
  72.8 2.7 copy-done.4
  75.5 8.2 %collective-permute-done.2 = bf16[256,1,8,256]{0,3,2,1:T(8,128)(2,1)} collective-permute-done((bf16[256,1,8,256]{0,3,2,1:T(8,128)(2,1)S(1)}, bf16[256,1,8,256]{0,3,2,1:T(8,128)(2,1)}, u32[]{:S(2)}, u32[]{:S(2)}) %collective-permute-start.2) | collective-permute-done | bytes 1048608 | tf_op jit(solution)/shard_map/ppermute | solution.py:14
  83.7 1.9 pad_maximum_fusion
  85.5 2.6 fusion.156
  88.1 2.5 fusion.157
  90.6 2.7 fusion.158
  93.4 3.0 fusion.159
  96.4 2.2 copy.112
  98.6 3.0 fusion.27
  101.6 2.4 fusion.26
  104.0 1.5 fusion.25
  105.5 1.5 fusion.24
  107.0 1.1 fusion.23
  108.2 2.2 copy.113
  110.4 2.2 copy.114
  112.6 3.0 fusion.22
  115.6 3.0 fusion.21
  118.6 1.1 fusion.20
  119.7 1.5 fusion.19
  121.2 1.5 fusion.18
  123.8 1.5 fusion.16
  125.3 1.5 fusion.15
  126.8 1.1 fusion.14
  128.0 2.2 copy.115
  130.2 2.2 copy.116
  132.4 3.0 fusion.13
  135.4 3.0 fusion.12
  138.4 1.1 fusion.11
  139.5 1.5 fusion.10
  141.0 1.5 fusion.9
  143.6 1.5 fusion.7
  145.1 1.5 fusion.6
  146.6 1.1 fusion.5
  147.8 1.8 copy.117
  149.6 2.9 fusion.4
  152.5 1.6 fusion.3
  155.2 1.5 fusion.1
  157.6 2.7 bitcast_dynamic-update-slice_fusion
  160.3 1.6 bitcast_dynamic-update-slice_fusion.10
  163.6 1.6 bitcast_dynamic-update-slice_fusion.8
  165.2 6.6 %copy.74 = bf16[9,128,1,2048]{3,1,0,2:T(8,128)(2,1)} copy(bf16[9,128,1,2048]{1,3,2,0:T(8,128)(2,1)} %get-tuple-element.73) | data formatting | bytes 9437184 | tf_op jit(solution)/shard_map/stack | solution.py:48
  171.8 6.7 %copy.76 = bf16[9,128,1,2048]{3,1,0,2:T(8,128)(2,1)} copy(bf16[9,128,1,2048]{1,3,2,0:T(8,128)(2,1)} %get-tuple-element.72) | data formatting | bytes 9437184 | tf_op jit(solution)/shard_map/stack | solution.py:48
  178.5 6.9 %copy.79 = bf16[9,128,1,2048]{3,1,0,2:T(8,128)(2,1)} copy(bf16[9,128,1,2048]{1,3,2,0:T(8,128)(2,1)} %get-tuple-element.62) | data formatting | bytes 9437184 | tf_op jit(solution)/shard_map/stack | solution.py:48
  185.4 4.2 %fusion.165 = f32[2048,256]{1,0:T(8,128)S(1)} fusion(bf16[1152,2048]{1,0:T(8,128)(2,1)} %bitcast.359, bf16[256,1152]{0,1:T(8,128)(2,1)S(1)} %bitcast.367), kind=kOutput, calls=%fused_computation.235 | convolution fusion | flops 1207959552 | bytes 7405568 | tf_op jit(solution)/shard_map/dot_general | solution.py:69
  189.6 1.7 convolution_add_fusion.1
  192.2 3.0 fusion
  195.3 102.3 %all-reduce.50.cloned.1.call-done = f32[27,256,128]{2,1,0:T(8,128)} async-done(((f32[27,256,128]{2,1,0:T(8,128)}), f32[27,256,128]{2,1,0:T(8,128)}) %all-reduce.50.cloned.1.call-update) | async-done | bytes 3538960 | tf_op jit(solution)/shard_map/psum | solution.py:95
  297.6 4.2 %broadcast_multiply_fusion = f32[27,256,128]{2,1,0:T(8,128)} fusion(f32[27,256,128]{2,1,0:T(8,128)} %all-reduce.50.cloned.1.call-done), kind=kLoop, calls=%fused_computation.4 | loop fusion | flops 884736 | bytes 7077888 | tf_op jit(solution)/shard_map/mul | solution.py:95
  301.7 1.3 convert_element_type.3
  303.0 1.2 copy.110
  (108 shorter events, 12.4 us)
Async XLA Ops:
  8.0 21.2 %copy-start.14 = (bf16[128,1,8,256]{3,2,1,0:T(8,128)(2,1)S(1)}, bf16[128,1,8,256]{3,2,1,0:T(8,128)(2,1)}, u32[]{:S(2)}) copy-start(bf16[128,1,8,256]{3,2,1,0:T(8,128)(2,1)} %param.4) | copy-start | bytes 1572868
  8.0 289.6 %all-reduce.50.cloned.1.call-start = ((), (), s32[]{:S(2)}) async-start(), calls=%async_computation.2 | async-start | bytes 7077888 | tf_op jit(solution)/shard_map/psum | solution.py:95
  10.3 21.0 %collective-permute-start.1 = (bf16[128,1,8,256]{0,3,2,1:T(8,128)(2,1)}, bf16[128,1,8,256]{0,3,2,1:T(8,128)(2,1)}, u32[]{:S(2)}, u32[]{:S(2)}) collective-permute-start(bf16[128,1,8,256]{0,3,2,1:T(8,128)(2,1)} %copy.71), channel_id=1, source_target_pairs={{2,0},{4,2},{6,4},{8,6},{10,8},{12,10},{14,12},{3,1},{5,3},{7,5},{... | collective-permute-start | bytes 1572872 | tf_op jit(solution)/shard_map/ppermute | solution.py:17
  11.6 49.8 %collective-permute-start = (bf16[128,1,8,256]{0,3,2,1:T(8,128)(2,1)}, bf16[128,1,8,256]{0,3,2,1:T(8,128)(2,1)}, u32[]{:S(2)}, u32[]{:S(2)}) collective-permute-start(bf16[128,1,8,256]{0,3,2,1:T(8,128)(2,1)} %copy.71), channel_id=1, source_target_pairs={{0,2},{2,4},{4,6},{6,8},{8,10},{10,12},{12,14},{1,3},{3,5},{5,7},{... | collective-permute-start | bytes 1572872 | tf_op jit(solution)/shard_map/ppermute | solution.py:14
  19.6 11.8 %copy-start.8 = (bf16[256,1,8,256]{0,3,2,1:T(8,128)(2,1)}, bf16[256,1,8,256]{0,3,2,1:T(8,128)(2,1)S(1)}, u32[]{:S(2)}) copy-start(bf16[256,1,8,256]{0,3,2,1:T(8,128)(2,1)S(1)} %copy.80) | copy-start | bytes 3145732
  19.6 53.2 %collective-permute-start.3 = (bf16[256,1,8,256]{0,3,2,1:T(8,128)(2,1)S(1)}, bf16[256,1,8,256]{0,3,2,1:T(8,128)(2,1)}, u32[]{:S(2)}, u32[]{:S(2)}) collective-permute-start(bf16[256,1,8,256]{0,3,2,1:T(8,128)(2,1)S(1)} %copy.80), channel_id=1, source_target_pairs={{2,0},{4,2},{6,4},{8,6},{10,8},{12,10},{14,12},{3,1},{5,3},{7,5},{... | collective-permute-start | bytes 3145736 | tf_op jit(solution)/shard_map/ppermute | solution.py:17
  20.9 62.8 %collective-permute-start.2 = (bf16[256,1,8,256]{0,3,2,1:T(8,128)(2,1)S(1)}, bf16[256,1,8,256]{0,3,2,1:T(8,128)(2,1)}, u32[]{:S(2)}, u32[]{:S(2)}) collective-permute-start(bf16[256,1,8,256]{0,3,2,1:T(8,128)(2,1)S(1)} %copy.80), channel_id=1, source_target_pairs={{0,2},{2,4},{4,6},{6,8},{8,10},{10,12},{12,14},{1,3},{3,5},{5,7},{... | collective-permute-start | bytes 3145736 | tf_op jit(solution)/shard_map/ppermute | solution.py:14
  70.8 12.8 %copy-start.9 = (bf16[256,1,8,256]{0,3,2,1:T(8,128)(2,1)S(1)}, bf16[256,1,8,256]{0,3,2,1:T(8,128)(2,1)}, u32[]{:S(2)}) copy-start(bf16[256,1,8,256]{0,3,2,1:T(8,128)(2,1)} %copy-done.8) | copy-start | bytes 3145732
  71.9 3.6 %copy-start.4 = (bf16[9,128,1,2048]{1,3,2,0:T(8,128)(2,1)}, bf16[9,128,1,2048]{1,3,2,0:T(8,128)(2,1)S(1)}, u32[]{:S(2)}) copy-start(bf16[9,128,1,2048]{1,3,2,0:T(8,128)(2,1)S(1)} %get-tuple-element.60) | copy-start | bytes 14155780
  71.9 11.8 %copy-start.6 = (bf16[9,128,1,2048]{1,3,2,0:T(8,128)(2,1)}, bf16[9,128,1,2048]{1,3,2,0:T(8,128)(2,1)S(1)}, u32[]{:S(2)}) copy-start(bf16[9,128,1,2048]{1,3,2,0:T(8,128)(2,1)S(1)} %get-tuple-element.61) | copy-start | bytes 14155780
  72.8 2.7 copy-start.5
  98.6 5.4 %copy-start = (bf16[16,8,8,256]{3,1,2,0:T(8,128)(2,1)S(1)}, bf16[16,8,8,256]{3,1,2,0:T(8,128)(2,1)}, u32[]{:S(2)}) copy-start(bf16[16,8,8,256]{3,1,2,0:T(8,128)(2,1)} %copy.118) | copy-start | bytes 1572868
  98.6 5.4 %copy-start.30 = (bf16[256,1,1793]{0,2,1:T(8,128)(2,1)S(1)}, bf16[256,1,1793]{0,2,1:T(8,128)(2,1)}, u32[]{:S(2)}) copy-start(bf16[256,1,1793]{0,2,1:T(8,128)(2,1)} %get-tuple-element.25) | copy-start | bytes 2754052
  98.6 6.9 %copy-start.26 = (bf16[256,1,2047]{0,2,1:T(8,128)(2,1)S(1)}, bf16[256,1,2047]{0,2,1:T(8,128)(2,1)}, u32[]{:S(2)}) copy-start(bf16[256,1,2047]{0,2,1:T(8,128)(2,1)} %get-tuple-element.31) | copy-start | bytes 3144196
  112.6 6.0 %copy-start.1 = (bf16[16,8,8,256]{3,1,2,0:T(8,128)(2,1)S(1)}, bf16[16,8,8,256]{3,1,2,0:T(8,128)(2,1)}, u32[]{:S(2)}) copy-start(bf16[16,8,8,256]{3,1,2,0:T(8,128)(2,1)} %copy.118) | copy-start | bytes 1572868
  112.6 6.0 %copy-start.12 = (bf16[256,1,1792]{2,0,1:T(8,128)(2,1)S(1)}, bf16[256,1,1792]{2,0,1:T(8,128)(2,1)}, u32[]{:S(2)}) copy-start(bf16[256,1,1792]{2,0,1:T(8,128)(2,1)} %copy.113) | copy-start | bytes 2752516
  112.6 7.1 %copy-start.35 = (bf16[256,1,1791]{0,2,1:T(8,128)(2,1)S(1)}, bf16[256,1,1791]{0,2,1:T(8,128)(2,1)}, u32[]{:S(2)}) copy-start(bf16[256,1,1791]{0,2,1:T(8,128)(2,1)} %get-tuple-element.12) | copy-start | bytes 2750980
  115.6 5.6 %copy-start.34 = (bf16[256,1,1791]{0,2,1:T(8,128)(2,1)S(1)}, bf16[256,1,1791]{0,2,1:T(8,128)(2,1)}, u32[]{:S(2)}) copy-start(bf16[256,1,1791]{0,2,1:T(8,128)(2,1)} %get-tuple-element.11) | copy-start | bytes 2750980
  118.6 4.2 %copy-start.10 = (bf16[256,1,1792]{2,0,1:T(8,128)(2,1)S(1)}, bf16[256,1,1792]{2,0,1:T(8,128)(2,1)}, u32[]{:S(2)}) copy-start(bf16[256,1,1792]{2,0,1:T(8,128)(2,1)} %copy.114) | copy-start | bytes 2752516
  119.7 4.2 %copy-start.29 = (bf16[256,1,1793]{0,2,1:T(8,128)(2,1)S(1)}, bf16[256,1,1793]{0,2,1:T(8,128)(2,1)}, u32[]{:S(2)}) copy-start(bf16[256,1,1793]{0,2,1:T(8,128)(2,1)} %get-tuple-element.23) | copy-start | bytes 2754052
  121.2 4.1 %copy-start.25 = (bf16[256,1,2047]{0,2,1:T(8,128)(2,1)S(1)}, bf16[256,1,2047]{0,2,1:T(8,128)(2,1)}, u32[]{:S(2)}) copy-start(bf16[256,1,2047]{0,2,1:T(8,128)(2,1)} %get-tuple-element.29) | copy-start | bytes 3144196
  132.4 6.0 %copy-start.2 = (bf16[16,8,8,256]{3,1,2,0:T(8,128)(2,1)S(1)}, bf16[16,8,8,256]{3,1,2,0:T(8,128)(2,1)}, u32[]{:S(2)}) copy-start(bf16[16,8,8,256]{3,1,2,0:T(8,128)(2,1)} %copy.118) | copy-start | bytes 1572868
  132.4 6.0 %copy-start.13 = (bf16[256,1,1792]{2,0,1:T(8,128)(2,1)S(1)}, bf16[256,1,1792]{2,0,1:T(8,128)(2,1)}, u32[]{:S(2)}) copy-start(bf16[256,1,1792]{2,0,1:T(8,128)(2,1)} %copy.115) | copy-start | bytes 2752516
  132.4 7.1 %copy-start.33 = (bf16[256,1,1791]{0,2,1:T(8,128)(2,1)S(1)}, bf16[256,1,1791]{0,2,1:T(8,128)(2,1)}, u32[]{:S(2)}) copy-start(bf16[256,1,1791]{0,2,1:T(8,128)(2,1)} %get-tuple-element.10) | copy-start | bytes 2750980
  135.4 5.6 %copy-start.32 = (bf16[256,1,1791]{0,2,1:T(8,128)(2,1)S(1)}, bf16[256,1,1791]{0,2,1:T(8,128)(2,1)}, u32[]{:S(2)}) copy-start(bf16[256,1,1791]{0,2,1:T(8,128)(2,1)} %get-tuple-element.9) | copy-start | bytes 2750980
  138.4 4.2 %copy-start.11 = (bf16[256,1,1792]{2,0,1:T(8,128)(2,1)S(1)}, bf16[256,1,1792]{2,0,1:T(8,128)(2,1)}, u32[]{:S(2)}) copy-start(bf16[256,1,1792]{2,0,1:T(8,128)(2,1)} %copy.116) | copy-start | bytes 2752516
  139.5 4.2 %copy-start.28 = (bf16[256,1,1793]{0,2,1:T(8,128)(2,1)S(1)}, bf16[256,1,1793]{0,2,1:T(8,128)(2,1)}, u32[]{:S(2)}) copy-start(bf16[256,1,1793]{0,2,1:T(8,128)(2,1)} %get-tuple-element.21) | copy-start | bytes 2754052
  141.0 4.1 %copy-start.24 = (bf16[256,1,2047]{0,2,1:T(8,128)(2,1)S(1)}, bf16[256,1,2047]{0,2,1:T(8,128)(2,1)}, u32[]{:S(2)}) copy-start(bf16[256,1,2047]{0,2,1:T(8,128)(2,1)} %get-tuple-element.27) | copy-start | bytes 3144196
  147.8 4.7 %copy-start.3 = (bf16[16,8,8,256]{3,1,2,0:T(8,128)(2,1)S(1)}, bf16[16,8,8,256]{3,1,2,0:T(8,128)(2,1)}, u32[]{:S(2)}) copy-start(bf16[16,8,8,256]{3,1,2,0:T(8,128)(2,1)} %copy.118) | copy-start | bytes 1572868
  147.8 4.7 %copy-start.27 = (bf16[256,1,1793]{0,2,1:T(8,128)(2,1)S(1)}, bf16[256,1,1793]{0,2,1:T(8,128)(2,1)}, u32[]{:S(2)}) copy-start(bf16[256,1,1793]{0,2,1:T(8,128)(2,1)} %get-tuple-element.20) | copy-start | bytes 2754052
  149.6 5.6 %copy-start.31 = (bf16[256,1,1791]{0,2,1:T(8,128)(2,1)S(1)}, bf16[256,1,1791]{0,2,1:T(8,128)(2,1)}, u32[]{:S(2)}) copy-start(bf16[256,1,1791]{0,2,1:T(8,128)(2,1)} %get-tuple-element.8) | copy-start | bytes 2750980
  154.1 2.7 copy-start.23
  155.2 2.4 copy-start.15
  155.2 2.4 copy-start.16
  156.6 3.7 %copy-start.17 = (bf16[128,1,1793]{0,2,1:T(8,128)(2,1)S(1)}, bf16[128,1,1793]{0,2,1:T(8,128)(2,1)}, u32[]{:S(2)}) copy-start(bf16[128,1,1793]{0,2,1:T(8,128)(2,1)} %get-tuple-element.49) | copy-start | bytes 1377028
  156.6 3.7 %copy-start.18 = (bf16[128,1,1793]{0,2,1:T(8,128)(2,1)S(1)}, bf16[128,1,1793]{0,2,1:T(8,128)(2,1)}, u32[]{:S(2)}) copy-start(bf16[128,1,1793]{0,2,1:T(8,128)(2,1)} %get-tuple-element.51) | copy-start | bytes 1377028
  156.7 5.2 %copy-start.22 = (bf16[128,1,1792]{0,2,1:T(8,128)(2,1)S(1)}, bf16[128,1,1792]{0,2,1:T(8,128)(2,1)}, u32[]{:S(2)}) copy-start(bf16[128,1,1792]{0,2,1:T(8,128)(2,1)} %get-tuple-element.43) | copy-start | bytes 1376260
  156.7 6.1 %copy-start.21 = (bf16[128,1,1792]{0,2,1:T(8,128)(2,1)S(1)}, bf16[128,1,1792]{0,2,1:T(8,128)(2,1)}, u32[]{:S(2)}) copy-start(bf16[128,1,1792]{0,2,1:T(8,128)(2,1)} %get-tuple-element.45) | copy-start | bytes 1376260
  156.7 145.1 %reduce-scatter.2.cloned.1.call-start = ((), (), s32[]{:S(2)}) async-start(), calls=%async_computation.1 | async-start | bytes 3145728 | tf_op jit(solution)/shard_map/reduce_scatter | solution.py:72
  157.6 6.0 %copy-start.19 = (bf16[128,1,1791]{0,2,1:T(8,128)(2,1)S(1)}, bf16[128,1,1791]{0,2,1:T(8,128)(2,1)}, u32[]{:S(2)}) copy-start(bf16[128,1,1791]{0,2,1:T(8,128)(2,1)} %get-tuple-element.37) | copy-start | bytes 1375492
  157.6 6.0 %copy-start.20 = (bf16[128,1,1791]{0,2,1:T(8,128)(2,1)S(1)}, bf16[128,1,1791]{0,2,1:T(8,128)(2,1)}, u32[]{:S(2)}) copy-start(bf16[128,1,1791]{0,2,1:T(8,128)(2,1)} %get-tuple-element.39) | copy-start | bytes 1375492
  178.5 6.9 %copy-start.38 = (bf16[256,9,128]{0,2,1:T(8,128)(2,1)S(1)}, bf16[256,9,128]{0,2,1:T(8,128)(2,1)}, u32[]{:S(2)}) copy-start(bf16[256,9,128]{0,2,1:T(8,128)(2,1)} %get-tuple-element.34) | copy-start | bytes 1769476
  178.5 11.1 %slice-start = ((s8[4718592]{0:T(1024)(128)(4,1)}), s8[524288]{0:T(1024)(128)(4,1)S(1)}, s32[]{:S(2)}) async-start(s8[4718592]{0:T(1024)(128)(4,1)} %bitcast.360), calls=%async_computation.3 | async-start | bytes 1048576
  185.4 4.2 %slice-start.1 = ((s8[4718592]{0:T(1024)(128)(4,1)}), s8[4194304]{0:T(1024)(128)(4,1)S(1)}, s32[]{:S(2)}) async-start(s8[4718592]{0:T(1024)(128)(4,1)} %bitcast.360), calls=%async_computation.4 | async-start | bytes 8388608
  185.4 4.2 %copy-start.37 = (bf16[256,9,128]{0,2,1:T(8,128)(2,1)S(1)}, bf16[256,9,128]{0,2,1:T(8,128)(2,1)}, u32[]{:S(2)}) copy-start(bf16[256,9,128]{0,2,1:T(8,128)(2,1)} %get-tuple-element.33) | copy-start | bytes 1769476
  189.6 2.4 copy-start.7
  189.6 2.6 copy-start.36
Sparse Core Ops, SparseCore 0:
  156.8 140.7 all-reduce.49
Sparse Core Ops, SparseCore 1:
  195.3 10.7 reduce-scatter.1
where the time goes:
time: 313 us; the launch traced here: 312 us
  waiting for transfers between devices  141 us (45%)
  local copies, waits for them, and re-layouts  65.7 us (21%)
  matrix products  56.2 us (18%)
  other arithmetic  18.9 us (6%)
  between operations  15.8 us (5%)
  starting transfers between devices  14.6 us (5%)
    psum x1, waiting for transfers between devices, local(): weight_grad = lax.psum(local_grad, 'gy') * norm_factor  102 us
    dot_general x27, matrix products, local(): lax.dot_general(moved, grad_flat, (((1,), (1,)), ((), ())), preferred_ele...  47.3 us
    ppermute x2, waiting for transfers between devices, padded(): lax.ppermute(lax.slice_in_dim(block, block.shape[dim] - width, None, axis...  38.2 us
    unnamed x99, local copies, waits for them, and re-layouts  28.2 us
    another operation x3, local copies, waits for them, and re-layouts, grad_group(): stacked = jnp.stack(pieces_list, 0)  20.2 us
    ppermute x2, starting transfers between devices, padded(): lax.ppermute(lax.slice_in_dim(block, block.shape[dim] - width, None, axis...  12 us
    slice x4, local copies, waits for them, and re-layouts, shift_cells(): moved = jnp.concatenate([flat[..., -offset:], filler], axis=-1)  10.8 us
    dot_general x3, matrix products, local(): jnp.dot(tap_cols, stacks[partial_y_off], preferred_element_type=jnp.float32)  8.93 us
  transfers between devices with their start and end apart: 6, of which 3 were waited for; matrix products, arithmetic and copies ran while one was open for 19% of the time, Pallas kernels for 0%

commit v1 on v0

v1 whole, which is shorter than its diff:
```python
import functools
import math

import jax
import jax.numpy as jnp
from jax import lax
from jax.experimental import pallas as pl
from jax.experimental.pallas import tpu as pltpu
from jax.sharding import PartitionSpec as P


def grads_kernel(x_count, high_ref, own_ref, low_ref, in_ref, w_ref, dg_ref, wg_ref, s_ref):
    out_count, cells = own_ref.shape
    s_ref[:, :x_count] = jnp.zeros((3 * out_count, x_count), s_ref.dtype)
    s_ref[:, x_count + cells :] = jnp.zeros((3 * out_count, x_count), s_ref.dtype)
    column = lax.broadcasted_iota(jnp.int32, (out_count, cells), 1) % x_count
    for order, a in enumerate((1, 0, 2)):
        plane = (high_ref, own_ref, low_ref)[a][...]
        wide = plane.astype(jnp.float32)
        left = jnp.where(column == x_count - 1, 0.0, pltpu.roll(wide, cells - 1, 1))
        right = jnp.where(column == 0, 0.0, pltpu.roll(wide, 1, 1))
        for c, moved in enumerate((left, wide, right)):
            s_ref[c * out_count : (c + 1) * out_count, x_count : x_count + cells] = moved.astype(
                s_ref.dtype
            )
        for b in range(3):
            window = s_ref[:, (2 - b) * x_count : (2 - b) * x_count + cells]
            taps = jnp.concatenate([w_ref[9 * a + 3 * b + c] for c in range(3)], axis=1)
            term = jnp.dot(taps, window, preferred_element_type=jnp.float32)
            if order == 0 and b == 0:
                dg_ref[...] = term
            else:
                dg_ref[...] += term
            grad = lax.dot_general(
                in_ref[...], window, (((1,), (1,)), ((), ())), preferred_element_type=jnp.float32
            )
            for c in range(3):
                wg_ref[9 * a + 3 * b + c] = grad[:, c * out_count : (c + 1) * out_count]


def local(inputs, cotangent, weight):
    channels, rows, z_count, x_count = inputs.shape
    out_count = cotangent.shape[0]
    cells = rows * z_count * x_count
    count = lax.axis_size("gy")
    forward = [(i, i + 1) for i in range(count - 1)]
    backward = [(target, source) for source, target in forward]
    own = cotangent.reshape(out_count, cells)
    low = lax.ppermute(own, "gy", forward)
    high = lax.ppermute(own, "gy", backward)
    summed, taps = pl.pallas_call(
        functools.partial(grads_kernel, x_count),
        out_shape=(
            jax.ShapeDtypeStruct((channels, cells), jnp.float32),
            jax.ShapeDtypeStruct((27, channels, out_count), jnp.float32),
        ),
        in_specs=[pl.BlockSpec(memory_space=pltpu.VMEM)] * 5,
        out_specs=[pl.BlockSpec(memory_space=pltpu.VMEM)] * 2,
        scratch_shapes=[pltpu.VMEM((3 * out_count, cells + 2 * x_count), jnp.bfloat16)],
        compiler_params=pltpu.CompilerParams(vmem_limit_bytes=48 * 2**20),
        name="grads",
    )(high, own, low, inputs.reshape(channels, cells), weight)
    grad_rows = lax.psum_scatter(summed, "ch", scatter_dimension=0, tiled=True)
    input_grad = grad_rows.astype(jnp.bfloat16).reshape(-1, rows, z_count, x_count)
    norm_factor = 1.0 / math.sqrt(cells * count)
    weight_grad = lax.psum(taps, "gy") * norm_factor
    return (input_grad, weight_grad)


def solution(mesh):
    placed = (P(None, "gy", "grp", None), P("ch", "gy", "grp", None), P(None, None, "ch"))
    return jax.shard_map(
        local,
        mesh=mesh,
        in_specs=placed,
        out_specs=(P("ch", "gy", "grp", None), P("grp", None, "ch")),
        check_vma=False,
    )
```

time: 313 us -> 205 us (0.65)
  local copies, waits for them, and re-layouts: 65.7 us -> 3.71 us
  matrix products: 56.2 us -> 0 us
  waiting for transfers between devices: 141 us -> 161 us
  other arithmetic: 18.9 us -> 5.46 us
  Pallas kernels: 0 us -> 12.3 us
  starting transfers between devices: 14.6 us -> 6.28 us
    dot_general x30 -> x0, matrix products: 56.2 us -> none  [the longest x27 47.3 us: local(): lax.dot_general(moved, grad_flat, (((1,), (1,)), ((), ())), preferred_ele...]
    psum x1, waiting for transfers between devices: 102 us -> 141 us  [local(): weight_grad = lax.psum(taps, 'gy') * norm_factor]
    unnamed x99 -> x5, local copies, waits for them, and re-layouts: 28.2 us -> 3.71 us
    another operation x3 -> x0, local copies, waits for them, and re-layouts: 20.2 us -> none  [grad_group(): stacked = jnp.stack(pieces_list, 0)]
    ppermute x4 -> x2, waiting for transfers between devices: 38.2 us -> 19.5 us  [the longest x1 19.5 us: local(): low = lax.ppermute(own, 'gy', forward)]
    slice x9 -> x0, local copies, waits for them, and re-layouts: 17.3 us -> none  [the longest x4 10.8 us: shift_cells(): moved = jnp.concatenate([flat[..., -offset:], filler], axis=-1)]
    pallas_call x0 -> x1, Pallas kernels: none -> 12.3 us  [local(): pl.pallas_call(functools.partial(grads_kernel, x_count), out_shape=(jax.S...]
    ppermute x4 -> x2, starting transfers between devices: 14.5 us -> 6.2 us  [the longest x1 4.9 us: local(): low = lax.ppermute(own, 'gy', forward)]
  transfers between devices with their start and end apart: 6 -> 4, of which waited for: 3 -> 2; matrix products, arithmetic and copies ran while one was open for 19% -> 3% of each run, Pallas kernels for 0% -> 0%
where the time goes in v1:
time: 205 us
  waiting for transfers between devices  161 us (79%)
  between operations  15.5 us (8%)
  Pallas kernels  12.3 us (6%)
  starting transfers between devices  6.28 us (3%)
  other arithmetic  5.46 us (3%)
  local copies, waits for them, and re-layouts  3.71 us (2%)
    psum x1, waiting for transfers between devices, local(): weight_grad = lax.psum(taps, 'gy') * norm_factor  141 us
    ppermute x1, waiting for transfers between devices, local(): low = lax.ppermute(own, 'gy', forward)  19.5 us
    pallas_call x1, Pallas kernels, local(): pl.pallas_call(functools.partial(grads_kernel, x_count), out_shape=(jax.S...  12.3 us
    ppermute x1, starting transfers between devices, local(): low = lax.ppermute(own, 'gy', forward)  4.9 us
    mul x1, other arithmetic, local(): weight_grad = lax.psum(taps, 'gy') * norm_factor  4.17 us
  transfers between devices with their start and end apart: 4, of which 2 were waited for; matrix products, arithmetic and copies ran while one was open for 3% of the time, Pallas kernels for 0%

profile of v1, /device:TPU:0, one launch (start us, length us, event | category | flops | bytes accessed | tf_op | source)
XLA Modules:
  0.0 204.5 jit_solution(9988615907019485761)
XLA Ops:
  8.0 0.0 copy-start
  8.0 0.0 all-reduce.2.cloned.1.call-start
  8.1 1.3 copy.6
  9.3 4.9 %collective-permute-start.1 = (bf16[128,2048]{1,0:T(8,128)(2,1)S(1)}, bf16[128,2048]{1,0:T(8,128)(2,1)S(1)}, u32[]{:S(2)}, u32[]{:S(2)}) collective-permute-start(bf16[128,2048]{1,0:T(8,128)(2,1)S(1)} %bitcast.13), channel_id=1, source_target_pairs={{0,2},{2,4},{4,6},{6,8},{8,10},{10,12},{12,14},{1,3},{3,5},{5,7},{... | collective-permute-start | bytes 1572872 | tf_op jit(solution)/shard_map/ppermute | solution.py:49
  14.2 1.3 collective-permute-start
  15.5 1.5 copy.7
  17.1 19.5 %collective-permute-done.1.low_ref = bf16[128,2048]{1,0:T(8,128)(2,1)S(1)} collective-permute-done((bf16[128,2048]{1,0:T(8,128)(2,1)S(1)}, bf16[128,2048]{1,0:T(8,128)(2,1)S(1)}, u32[]{:S(2)}, u32[]{:S(2)}) %collective-permute-start.1) | collective-permute-done | bytes 524320 | tf_op jit(solution)/shard_map/ppermute | solution.py:49
  36.6 0.0 collective-permute-done.high_ref
  36.6 0.0 copy-done
  36.6 12.3 %grads.1 = (f32[256,2048]{1,0:T(8,128)}, f32[27,256,128]{2,1,0:T(8,128)}) custom-call(bf16[128,2048]{1,0:T(8,128)(2,1)S(1)} %collective-permute-done.high_ref, bf16[128,2048]{1,0:T(8,128)(2,1)S(1)} %bitcast.15, bf16[128,2048]{1,0:T(8,128)(2,1)S(1)} %collective-permute-done.1.low_ref, bf16[256,2048]{1,0:T(8,128)(2,1)S(1)} %bitcast.12, ...), custom_call_target="tpu_custom_call" | custom-call | tf_op jit(solution)/shard_map/grads/pallas_call | solution.py:51
  48.9 0.0 all-reduce.2.cloned.1.call-update
  49.0 0.0 reduce-scatter.2.cloned.1.call-start
  49.0 0.5 reduce-scatter.2.cloned.1.call-update
  49.6 141.2 %all-reduce.2.cloned.1.call-done = f32[27,256,128]{2,1,0:T(8,128)} async-done(((f32[27,256,128]{2,1,0:T(8,128)}), f32[27,256,128]{2,1,0:T(8,128)}) %all-reduce.2.cloned.1.call-update) | async-done | bytes 3538960 | tf_op jit(solution)/shard_map/psum | solution.py:66
  190.7 4.2 %broadcast_multiply_fusion = f32[27,256,128]{2,1,0:T(8,128)} fusion(f32[27,256,128]{2,1,0:T(8,128)} %all-reduce.2.cloned.1.call-done), kind=kLoop, calls=%fused_computation | loop fusion | flops 884736 | bytes 7077888 | tf_op jit(solution)/shard_map/mul | solution.py:66
  194.9 0.0 reduce-scatter.2.cloned.1.call-done
  194.9 1.3 convert_element_type.3
  196.2 0.9 copy.8
Async XLA Ops:
  8.0 28.6 %copy-start = (bf16[27,256,128]{2,1,0:T(8,128)(2,1)S(1)}, bf16[27,256,128]{2,1,0:T(8,128)(2,1)}, u32[]{:S(2)}) copy-start(bf16[27,256,128]{2,1,0:T(8,128)(2,1)} %w_ref.1) | copy-start | bytes 5308420
  8.0 182.7 %all-reduce.2.cloned.1.call-start = ((), (), s32[]{:S(2)}) async-start(), calls=%async_computation.2 | async-start | bytes 7077888 | tf_op jit(solution)/shard_map/psum | solution.py:66
  9.3 27.3 %collective-permute-start.1 = (bf16[128,2048]{1,0:T(8,128)(2,1)S(1)}, bf16[128,2048]{1,0:T(8,128)(2,1)S(1)}, u32[]{:S(2)}, u32[]{:S(2)}) collective-permute-start(bf16[128,2048]{1,0:T(8,128)(2,1)S(1)} %bitcast.13), channel_id=1, source_target_pairs={{0,2},{2,4},{4,6},{6,8},{8,10},{10,12},{12,14},{1,3},{3,5},{5,7},{... | collective-permute-start | bytes 1572872 | tf_op jit(solution)/shard_map/ppermute | solution.py:49
  14.2 22.4 %collective-permute-start = (bf16[128,2048]{1,0:T(8,128)(2,1)S(1)}, bf16[128,2048]{1,0:T(8,128)(2,1)S(1)}, u32[]{:S(2)}, u32[]{:S(2)}) collective-permute-start(bf16[128,2048]{1,0:T(8,128)(2,1)S(1)} %bitcast.14), channel_id=1, source_target_pairs={{2,0},{4,2},{6,4},{8,6},{10,8},{12,10},{14,12},{3,1},{5,3},{7,5},{... | collective-permute-start | bytes 1572872 | tf_op jit(solution)/shard_map/ppermute | solution.py:50
  49.0 145.9 %reduce-scatter.2.cloned.1.call-start = ((), (), s32[]{:S(2)}) async-start(), calls=%async_computation.1 | async-start | bytes 3145728 | tf_op jit(solution)/shard_map/reduce_scatter | solution.py:63
Sparse Core Ops, SparseCore 0:
  49.1 141.5 all-reduce.1
Sparse Core Ops, SparseCore 1:
  51.7 11.7 reduce-scatter.1

commit v2 on v1

v2 whole, which is shorter than its diff:
```python
import functools
import math

import jax
import jax.numpy as jnp
from jax import lax
from jax.experimental import pallas as pl
from jax.experimental.pallas import tpu as pltpu
from jax.sharding import PartitionSpec as P

MESH = pl.DeviceIdType.MESH
SPAN = 166.0
PLANES = (1, 0, 2)
GROUPS = tuple((a, b) for a in PLANES for b in range(3))


def encode(values):
    top = jnp.max(jnp.abs(values), axis=0, keepdims=True)
    scale = (top * 1.01 + 1e-30).astype(jnp.bfloat16)
    size = jnp.exp(jnp.abs(values) * (SPAN / scale.astype(jnp.float32)) - SPAN / 2)
    code = jnp.where(values < 0, -size, size).astype(jnp.bfloat16)
    return code, jnp.broadcast_to(scale, (16, values.shape[1]))


def decode(code, scale):
    wide = code.astype(jnp.float32)
    step = scale.astype(jnp.float32)[0:1] * (1.0 / SPAN)
    size = (jnp.log(jnp.abs(wide)) + SPAN / 2) * step
    return jnp.where(wide < 0, -size, size)


def grads_kernel(
    x_count, count, norm, own_ref, in_ref, w_ref, out_ref, wg_ref,
    halo, s_ref, dg, dg_in, part, y_out, y_in, half, z_out, z_in, own_f, other_f,
    halo_s, halo_r, y_s, y_r, z_s, z_r, f_s, f_r, g_s, g_r, c_s, c_r,
):
    out_count, cells = own_ref.shape
    channels = in_ref.shape[0]
    me = lax.axis_index("gy")
    core = lax.axis_index("ch")
    parity = lax.rem(me, 2)
    place = lax.div(me, 2)
    partner = me + 1 - 2 * parity
    line = count // 2
    full = 3 * channels // 2
    per = z_out.shape[2] - 16

    def along(d):
        return 2 * lax.rem(place + d, line) + parity

    def copy(src, dst, send, recv, **where):
        return pltpu.make_async_remote_copy(
            src_ref=src, dst_ref=dst, send_sem=send, recv_sem=recv,
            device_id=where, device_id_type=MESH,
        )

    barrier = pltpu.get_barrier_semaphore()
    for d in range(1, count):
        pl.semaphore_signal(
            barrier, inc=1, device_id={"gy": lax.rem(me + d, count)}, device_id_type=MESH
        )
    pl.semaphore_signal(barrier, inc=1, device_id={"ch": 1 - core}, device_id_type=MESH)
    pl.semaphore_wait(barrier, count)

    down = copy(own_ref, halo.at[0], halo_s.at[0], halo_r.at[0], gy=jnp.maximum(me - 1, 0))
    up = copy(own_ref, halo.at[1], halo_s.at[1], halo_r.at[1], gy=jnp.minimum(me + 1, count - 1))

    @pl.when(me > 0)
    def _():
        down.start()

    @pl.when(me < count - 1)
    def _():
        up.start()

    @pl.when(me == 0)
    def _():
        halo[1] = jnp.zeros((out_count, cells), halo.dtype)

    @pl.when(me == count - 1)
    def _():
        halo[0] = jnp.zeros((out_count, cells), halo.dtype)

    y_copies = [
        copy(y_out.at[g], y_in.at[g], y_s.at[g], y_r.at[g], gy=partner) for g in range(9)
    ]
    z_copies = [
        [
            copy(z_out.at[g, d - 1], z_in.at[g, d - 1], z_s.at[g, d - 1], z_r.at[g, d - 1],
                 gy=along(d))
            for d in range(1, line)
        ]
        for g in range(9)
    ]
    f_copies = [
        [
            copy(own_f.at[g, place], own_f.at[g, place], f_s.at[g, d - 1], f_r.at[g, d - 1],
                 gy=along(d))
            for d in range(1, line)
        ]
        for g in range(9)
    ]
    g_copies = [
        copy(own_f.at[g], other_f.at[g], g_s.at[g], g_r.at[g], gy=partner) for g in range(9)
    ]

    def shift(a):
        if a == 0:
            plane = halo[0]
        elif a == 1:
            plane = own_ref[...]
        else:
            plane = halo[1]
        column = lax.broadcasted_iota(jnp.int32, (out_count, cells), 1) % x_count
        wide = plane.astype(jnp.float32)
        left = jnp.where(column == x_count - 1, 0.0, pltpu.roll(wide, cells - 1, 1))
        right = jnp.where(column == 0, 0.0, pltpu.roll(wide, 1, 1))
        edge = jnp.zeros((3 * out_count, x_count), s_ref.dtype)
        s_ref[a, :, :x_count] = edge
        s_ref[a, :, x_count + cells :] = edge
        for c, moved in enumerate((left, plane, right)):
            s_ref[a, c * out_count : (c + 1) * out_count, x_count : x_count + cells] = (
                moved.astype(s_ref.dtype)
            )

    def window(a, b):
        return s_ref[a, :, (2 - b) * x_count : (2 - b) * x_count + cells]

    def produce(g):
        grad = lax.dot_general(
            in_ref[...], window(*GROUPS[g]), (((1,), (1,)), ((), ())),
            preferred_element_type=jnp.float32,
        )
        for c in range(3):
            part[g, c * channels : (c + 1) * channels, :] = grad[
                :, c * out_count : (c + 1) * out_count
            ]
        code, scale = encode(part[g, pl.ds((1 - parity) * full, full), :])
        y_out[g, :full] = code
        y_out[g, full:] = scale
        y_copies[g].start()

    def spread(g):
        y_copies[g].wait_recv()
        half[g, :full] = part[g, pl.ds(parity * full, full), :] + decode(
            y_in[g, :full], y_in[g, full:]
        )
        if line * per > full:
            half[g, full:] = jnp.zeros((line * per - full, out_count), half.dtype)
        for d in range(1, line):
            target = lax.rem(place + d, line)
            code, scale = encode(half[g, pl.ds(target * per, per), :])
            z_out[g, d - 1, :per] = code
            z_out[g, d - 1, per:] = scale
            z_copies[g][d - 1].start()

    def collect(g):
        total = half[g, pl.ds(place * per, per), :]
        for d in range(1, line):
            z_copies[g][d - 1].wait_recv()
            total = total + decode(z_in[g, d - 1, :per], z_in[g, d - 1, per:])
        code, scale = encode(total * norm)
        own_f[g, place, :per] = code
        own_f[g, place, per:] = scale
        for d in range(1, line):
            f_copies[g][d - 1].start()

    def forward(g):
        for d in range(1, line):
            f_copies[g][d - 1].wait_recv()
        g_copies[g].start()

    def place_half(g, source, side):
        a, b = GROUPS[g]
        base = (9 * a + 3 * b) * channels
        for j in range(line):
            rows = min(per, full - j * per)
            if rows > 0:
                wg_ref[pl.ds(base + side * full + j * per, rows), :] = decode(
                    source[g, j, :rows], source[g, j, per:]
                )

    def finish(g):
        g_copies[g].wait_recv()
        place_half(g, other_f, 1 - parity)

    def dgrad(a):
        terms = None
        for b in range(3):
            taps = jnp.concatenate([w_ref[9 * a + 3 * b + c] for c in range(3)], axis=1)
            term = jnp.dot(taps, window(a, b), preferred_element_type=jnp.float32)
            terms = term if b == 0 else terms + term
        if a == PLANES[0]:
            dg[...] = terms
        else:
            dg[...] += terms

    owned = channels // 2
    shift(1)
    for g in range(3):
        produce(g)
    dgrad(1)

    @pl.when(me < count - 1)
    def _():
        down.wait_recv()

    shift(0)
    for g in range(3, 6):
        produce(g)
    for g in range(3):
        spread(g)

    @pl.when(me > 0)
    def _():
        up.wait_recv()

    shift(2)
    for g in range(6, 9):
        produce(g)
    for g in range(3):
        collect(g)
    dgrad(0)
    for g in range(3, 6):
        spread(g)
    for g in range(3):
        forward(g)
    dgrad(2)
    to_core = copy(dg.at[pl.ds((1 - core) * owned, owned)], dg_in, c_s, c_r, ch=1 - core)
    to_core.start()
    for g in range(3):
        spread(g + 6)
        collect(g + 3)
        place_half(g, own_f, parity)
    for g in range(3):
        collect(g + 6)
        forward(g + 3)
        finish(g)
        place_half(g + 3, own_f, parity)
    to_core.wait_recv()
    out_ref[...] = (dg[pl.ds(core * owned, owned), :] + dg_in[...]).astype(out_ref.dtype)
    for g in range(3):
        forward(g + 6)
        finish(g + 3)
        place_half(g + 6, own_f, parity)
    for g in range(6, 9):
        finish(g)

    @pl.when(me > 0)
    def _():
        down.wait_send()

    @pl.when(me < count - 1)
    def _():
        up.wait_send()

    to_core.wait_send()
    for g in range(9):
        y_copies[g].wait_send()
        g_copies[g].wait_send()
        for d in range(1, line):
            z_copies[g][d - 1].wait_send()
            f_copies[g][d - 1].wait_send()


def local(inputs, cotangent, weight):
    channels, rows, z_count, x_count = inputs.shape
    out_count = cotangent.shape[0]
    cells = rows * z_count * x_count
    count = lax.axis_size("gy")
    line = count // 2
    full = 3 * channels // 2
    per = -(-full // (line * 16)) * 16
    norm = 1.0 / math.sqrt(cells * count)
    bf16, f32 = jnp.bfloat16, jnp.float32
    dma = pltpu.SemaphoreType.DMA
    input_grad, weight_grad = pl.pallas_call(
        functools.partial(grads_kernel, x_count, count, norm),
        out_shape=(
            jax.ShapeDtypeStruct((channels // 2, cells), bf16),
            jax.ShapeDtypeStruct((27 * channels, out_count), f32),
        ),
        in_specs=[pl.BlockSpec(memory_space=pltpu.VMEM)] * 3,
        out_specs=[pl.BlockSpec(memory_space=pltpu.VMEM)] * 2,
        scratch_shapes=[
            pltpu.VMEM((2, out_count, cells), bf16),
            pltpu.VMEM((3, 3 * out_count, cells + 2 * x_count), bf16),
            pltpu.VMEM((channels, cells), f32),
            pltpu.VMEM((channels // 2, cells), f32),
            pltpu.VMEM((9, 3 * channels, out_count), f32),
            pltpu.VMEM((9, full + 16, out_count), bf16),
            pltpu.VMEM((9, full + 16, out_count), bf16),
            pltpu.VMEM((9, line * per, out_count), f32),
            pltpu.VMEM((9, line - 1, per + 16, out_count), bf16),
            pltpu.VMEM((9, line - 1, per + 16, out_count), bf16),
            pltpu.VMEM((9, line, per + 16, out_count), bf16),
            pltpu.VMEM((9, line, per + 16, out_count), bf16),
            dma((2,)),
            dma((2,)),
            dma((9,)),
            dma((9,)),
            dma((9, line - 1)),
            dma((9, line - 1)),
            dma((9, line - 1)),
            dma((9, line - 1)),
            dma((9,)),
            dma((9,)),
            dma(()),
            dma(()),
        ],
        compiler_params=pltpu.CompilerParams(
            collective_id=0, has_side_effects=True, vmem_limit_bytes=56 * 2**20
        ),
        name="grads",
    )(cotangent.reshape(out_count, cells), inputs.reshape(channels, cells), weight)
    return (
        input_grad.reshape(-1, rows, z_count, x_count),
        weight_grad.reshape(27, channels, out_count),
    )


def solution(mesh):
    placed = (P(None, "gy", "grp", None), P("ch", "gy", "grp", None), P(None, None, "ch"))
    return jax.shard_map(
        local,
        mesh=mesh,
        in_specs=placed,
        out_specs=(P("ch", "gy", "grp", None), P("grp", None, "ch")),
        check_vma=False,
    )
```

time: 205 us -> 99.8 us (0.49)
  waiting for transfers between devices: 161 us -> 0 us
  Pallas kernels: 12.3 us -> 87.9 us
  between operations: 15.5 us -> 0.64 us
  local copies, waits for them, and re-layouts: 3.71 us -> 10.6 us
  starting transfers between devices: 6.28 us -> 0 us
  other arithmetic: 5.46 us -> 0 us
    psum x1 -> x0, waiting for transfers between devices: 141 us -> none  [local(): weight_grad = lax.psum(taps, 'gy') * norm_factor]
    pallas_call x1, Pallas kernels: 12.3 us -> 87.9 us  [local(): pl.pallas_call(functools.partial(grads_kernel, x_count, count, norm), out...]
    ppermute x2 -> x0, waiting for transfers between devices: 19.5 us -> none  [the longest x1 19.5 us: local(): low = lax.ppermute(own, 'gy', forward)]
    unnamed x5 -> x4, local copies, waits for them, and re-layouts: 3.71 us -> 10.6 us
    ppermute x2 -> x0, starting transfers between devices: 6.2 us -> none  [the longest x1 4.9 us: local(): low = lax.ppermute(own, 'gy', forward)]
    mul x1 -> x0, other arithmetic: 4.17 us -> none  [local(): weight_grad = lax.psum(taps, 'gy') * norm_factor]
  transfers between devices with their start and end apart: 4 -> 0, of which waited for: 2 -> 0; matrix products, arithmetic and copies ran while one was open for 3% -> 0% of each run, Pallas kernels for 0% -> 0%
where the time goes in v2:
time: 99.8 us; the launch traced here: 99.2 us
  Pallas kernels  87.9 us (88%)
  local copies, waits for them, and re-layouts  10.6 us (11%)
    pallas_call x1, Pallas kernels, local(): pl.pallas_call(functools.partial(grads_kernel, x_count, count, norm), out...  87.9 us
    unnamed x4, local copies, waits for them, and re-layouts  10.6 us

profile of v2, /device:TPU:0, one launch (start us, length us, event | category | flops | bytes accessed | tf_op | source)
XLA Modules:
  0.0 99.2 jit_solution(11392822695042706910)
XLA Ops:
  0.6 2.0 %copy.6 = bf16[16,8,8,256]{3,1,2,0:T(8,128)(2,1)} copy(bf16[16,8,8,256]{3,2,1,0:T(8,128)(2,1)} %bitcast.17) | data formatting | bytes 1048576
  2.6 2.5 %copy.7 = bf16[32,8,8,256]{3,1,2,0:T(8,128)(2,1)} copy(bf16[32,8,8,256]{3,2,1,0:T(8,128)(2,1)} %bitcast.16) | data formatting | bytes 2097152
  5.1 87.9 %grads.1 = (bf16[128,2048]{1,0:T(8,128)(2,1)}, f32[6912,128]{1,0:T(8,128)}) custom-call(bf16[128,2048]{1,0:T(8,128)(2,1)} %bitcast.15, bf16[256,2048]{1,0:T(8,128)(2,1)} %bitcast.13, bf16[27,256,128]{2,1,0:T(8,128)(2,1)} %w_ref.1), custom_call_target="tpu_custom_call" | custom-call | tf_op jit(solution)/shard_map/grads/pallas_call | solution.py:277
  93.0 2.0 %copy.8 = bf16[16,8,8,256]{3,2,1,0:T(8,128)(2,1)} copy(bf16[16,8,8,256]{3,1,2,0:T(8,128)(2,1)} %bitcast.19) | data formatting | bytes 1048576
  95.0 4.2 %copy.10 = f32[27,256,128]{2,1,0:T(8,128)} copy(f32[27,256,128]{2,1,0:T(8,128)} %bitcast.14) | data formatting | bytes 7077888

commit v3 on v2

--- a/solution.py
+++ b/solution.py
@@ -31,7 +31,7 @@
 
 def grads_kernel(
     x_count, count, norm, own_ref, in_ref, w_ref, out_ref, wg_ref,
-    halo, s_ref, dg, dg_in, part, y_out, y_in, half, z_out, z_in, own_f, other_f,
+    halo, s_ref, dg, dg_in, part, y_out, y_in, half, zz_out, zz_in, z_out, z_in, done,
     halo_s, halo_r, y_s, y_r, z_s, z_r, f_s, f_r, g_s, g_r, c_s, c_r,
 ):
     out_count, cells = own_ref.shape
@@ -69,10 +69,6 @@
     def _():
         down.start()
 
-    @pl.when(me < count - 1)
-    def _():
-        up.start()
-
     @pl.when(me == 0)
     def _():
         halo[1] = jnp.zeros((out_count, cells), halo.dtype)
@@ -81,27 +77,30 @@
     def _():
         halo[0] = jnp.zeros((out_count, cells), halo.dtype)
 
+    early = len(zz_out)
+    lot = [slice(0, per + 16) if g < early else slice(None) for g in range(9)]
     y_copies = [
-        copy(y_out.at[g], y_in.at[g], y_s.at[g], y_r.at[g], gy=partner) for g in range(9)
-    ]
-    z_copies = [
-        [
-            copy(z_out.at[g, d - 1], z_in.at[g, d - 1], z_s.at[g, d - 1], z_r.at[g, d - 1],
-                 gy=along(d))
-            for d in range(1, line)
-        ]
+        copy(y_out.at[g, lot[g]], y_in.at[g, lot[g]], y_s.at[g], y_r.at[g], gy=partner)
         for g in range(9)
     ]
-    f_copies = [
-        [
-            copy(own_f.at[g, place], own_f.at[g, place], f_s.at[g, d - 1], f_r.at[g, d - 1],
-                 gy=along(d))
+    z_copies = []
+    f_copies = []
+    for g in range(9):
+        source, target = (zz_out, zz_in) if g < early else (z_out, z_in)
+        slot = g if g < early else g - early
+        z_copies.append([
+            copy(source.at[slot, d - 1], target.at[slot, d - 1],
+                 z_s.at[g, d - 1], z_r.at[g, d - 1], gy=along(d))
             for d in range(1, line)
-        ]
+        ])
+        mine = done.at[g, parity, place]
+        f_copies.append([
+            copy(mine, mine, f_s.at[g, d - 1], f_r.at[g, d - 1], gy=along(d))
+            for d in range(1, line)
+        ])
+    g_copies = [
+        copy(done.at[g, parity], done.at[g, parity], g_s.at[g], g_r.at[g], gy=partner)
         for g in range(9)
-    ]
-    g_copies = [
-        copy(own_f.at[g], other_f.at[g], g_s.at[g], g_r.at[g], gy=partner) for g in range(9)
     ]
 
     def shift(a):
@@ -131,37 +130,68 @@
             in_ref[...], window(*GROUPS[g]), (((1,), (1,)), ((), ())),
             preferred_element_type=jnp.float32,
         )
-        for c in range(3):
-            part[g, c * channels : (c + 1) * channels, :] = grad[
-                :, c * out_count : (c + 1) * out_count
-            ]
-        code, scale = encode(part[g, pl.ds((1 - parity) * full, full), :])
-        y_out[g, :full] = code
-        y_out[g, full:] = scale
-        y_copies[g].start()
+        first, second, third = (
+            grad[:, c * out_count : (c + 1) * out_count] for c in range(3)
+        )
+        middle = channels // 2
+        part[g, 0, :channels] = first
+        part[g, 0, channels:full] = second[:middle]
+        part[g, 1, :middle] = second[middle:]
+        part[g, 1, middle:full] = third
+        if line * per > full:
+            part[g, :, full:] = jnp.zeros((2, line * per - full, out_count), part.dtype)
+        if g < early:
+            for d in range(1, line):
+                target = lax.rem(place + d, line)
+                for side in range(2):
+                    code, scale = encode(part[g, side, pl.ds(target * per, per), :])
+                    zz_out[g, d - 1, side, :per] = code
+                    zz_out[g, d - 1, side, per:] = scale
+                z_copies[g][d - 1].start()
+        else:
+            code, scale = encode(part[g, 1 - parity, :full])
+            y_out[g, :full] = code
+            y_out[g, full:] = scale
+            y_copies[g].start()
 
     def spread(g):
-        y_copies[g].wait_recv()
-        half[g, :full] = part[g, pl.ds(parity * full, full), :] + decode(
-            y_in[g, :full], y_in[g, full:]
-        )
-        if line * per > full:
-            half[g, full:] = jnp.zeros((line * per - full, out_count), half.dtype)
-        for d in range(1, line):
-            target = lax.rem(place + d, line)
-            code, scale = encode(half[g, pl.ds(target * per, per), :])
-            z_out[g, d - 1, :per] = code
-            z_out[g, d - 1, per:] = scale
-            z_copies[g][d - 1].start()
+        if g < early:
+            totals = [part[g, side, pl.ds(place * per, per), :] for side in (parity, 1 - parity)]
+            for d in range(1, line):
+                z_copies[g][d - 1].wait_recv()
+                for n, side in enumerate((parity, 1 - parity)):
+                    totals[n] += decode(
+                        zz_in[g, d - 1, side, :per], zz_in[g, d - 1, side, per:]
+                    )
+            half[g, pl.ds(place * per, per), :] = totals[0]
+            code, scale = encode(totals[1])
+            y_out[g, :per] = code
+            y_out[g, per : per + 16] = scale
+            y_copies[g].start()
+        else:
+            y_copies[g].wait_recv()
+            half[g, :full] = part[g, parity, :full] + decode(y_in[g, :full], y_in[g, full:])
+            if line * per > full:
+                half[g, full:] = jnp.zeros((line * per - full, out_count), half.dtype)
+            for d in range(1, line):
+                target = lax.rem(place + d, line)
+                code, scale = encode(half[g, pl.ds(target * per, per), :])
+                z_out[g - early, d - 1, :per] = code
+                z_out[g - early, d - 1, per:] = scale
+                z_copies[g][d - 1].start()
 
     def collect(g):
         total = half[g, pl.ds(place * per, per), :]
-        for d in range(1, line):
-            z_copies[g][d - 1].wait_recv()
-            total = total + decode(z_in[g, d - 1, :per], z_in[g, d - 1, per:])
+        if g < early:
+            y_copies[g].wait_recv()
+            total = total + decode(y_in[g, :per], y_in[g, per : per + 16])
+        else:
+            for d in range(1, line):
+                z_copies[g][d - 1].wait_recv()
+                total = total + decode(z_in[g - early, d - 1, :per], z_in[g - early, d - 1, per:])
         code, scale = encode(total * norm)
-        own_f[g, place, :per] = code
-        own_f[g, place, per:] = scale
+        done[g, parity, place, :per] = code
+        done[g, parity, place, per:] = scale
         for d in range(1, line):
             f_copies[g][d - 1].start()
 
@@ -170,19 +200,10 @@
             f_copies[g][d - 1].wait_recv()
         g_copies[g].start()
 
-    def place_half(g, source, side):
+    def finish(g):
         a, b = GROUPS[g]
-        base = (9 * a + 3 * b) * channels
-        for j in range(line):
-            rows = min(per, full - j * per)
-            if rows > 0:
-                wg_ref[pl.ds(base + side * full + j * per, rows), :] = decode(
-                    source[g, j, :rows], source[g, j, per:]
-                )
-
-    def finish(g):
         g_copies[g].wait_recv()
-        place_half(g, other_f, 1 - parity)
+        wg_ref[3 * a + b] = done[g]
 
     def dgrad(a):
         terms = None
@@ -203,6 +224,7 @@
 
     @pl.when(me < count - 1)
     def _():
+        up.start()
         down.wait_recv()
 
     shift(0)
@@ -210,6 +232,7 @@
         produce(g)
     for g in range(3):
         spread(g)
+    dgrad(0)
 
     @pl.when(me > 0)
     def _():
@@ -220,29 +243,23 @@
         produce(g)
     for g in range(3):
         collect(g)
-    dgrad(0)
-    for g in range(3, 6):
-        spread(g)
-    for g in range(3):
-        forward(g)
+        spread(g + 3)
     dgrad(2)
     to_core = copy(dg.at[pl.ds((1 - core) * owned, owned)], dg_in, c_s, c_r, ch=1 - core)
     to_core.start()
     for g in range(3):
+        forward(g)
+        collect(g + 3)
         spread(g + 6)
-        collect(g + 3)
-        place_half(g, own_f, parity)
-    for g in range(3):
+    for g in range(3):
+        forward(g + 3)
         collect(g + 6)
-        forward(g + 3)
-        finish(g)
-        place_half(g + 3, own_f, parity)
     to_core.wait_recv()
     out_ref[...] = (dg[pl.ds(core * owned, owned), :] + dg_in[...]).astype(out_ref.dtype)
-    for g in range(3):
-        forward(g + 6)
-        finish(g + 3)
-        place_half(g + 6, own_f, parity)
+    for g in range(6):
+        finish(g)
+    for g in range(6, 9):
+        forward(g)
     for g in range(6, 9):
         finish(g)
 
@@ -274,11 +291,11 @@
     norm = 1.0 / math.sqrt(cells * count)
     bf16, f32 = jnp.bfloat16, jnp.float32
     dma = pltpu.SemaphoreType.DMA
-    input_grad, weight_grad = pl.pallas_call(
+    input_grad, codes = pl.pallas_call(
         functools.partial(grads_kernel, x_count, count, norm),
         out_shape=(
             jax.ShapeDtypeStruct((channels // 2, cells), bf16),
-            jax.ShapeDtypeStruct((27 * channels, out_count), f32),
+            jax.ShapeDtypeStruct((9, 2, line, per + 16, out_count), bf16),
         ),
         in_specs=[pl.BlockSpec(memory_space=pltpu.VMEM)] * 3,
         out_specs=[pl.BlockSpec(memory_space=pltpu.VMEM)] * 2,
@@ -287,14 +304,15 @@
             pltpu.VMEM((3, 3 * out_count, cells + 2 * x_count), bf16),
             pltpu.VMEM((channels, cells), f32),
             pltpu.VMEM((channels // 2, cells), f32),
-            pltpu.VMEM((9, 3 * channels, out_count), f32),
+            pltpu.VMEM((9, 2, line * per, out_count), f32),
             pltpu.VMEM((9, full + 16, out_count), bf16),
             pltpu.VMEM((9, full + 16, out_count), bf16),
             pltpu.VMEM((9, line * per, out_count), f32),
-            pltpu.VMEM((9, line - 1, per + 16, out_count), bf16),
-            pltpu.VMEM((9, line - 1, per + 16, out_count), bf16),
-            pltpu.VMEM((9, line, per + 16, out_count), bf16),
-            pltpu.VMEM((9, line, per + 16, out_count), bf16),
+            pltpu.VMEM((3, line - 1, 2, per + 16, out_count), bf16),
+            pltpu.VMEM((3, line - 1, 2, per + 16, out_count), bf16),
+            pltpu.VMEM((6, line - 1, per + 16, out_count), bf16),
+            pltpu.VMEM((6, line - 1, per + 16, out_count), bf16),
+            pltpu.VMEM((9, 2, line, per + 16, out_count), bf16),
             dma((2,)),
             dma((2,)),
             dma((9,)),
@@ -313,6 +331,10 @@
         ),
         name="grads",
     )(cotangent.reshape(out_count, cells), inputs.reshape(channels, cells), weight)
+    wide = codes[..., :per, :].astype(f32)
+    step = codes[..., per : per + 1, :].astype(f32) * (1.0 / SPAN)
+    size = (jnp.log(jnp.abs(wide)) + SPAN / 2) * step
+    weight_grad = jnp.where(wide < 0, -size, size).reshape(9, 2, line * per, out_count)[:, :, :full]
     return (
         input_grad.reshape(-1, rows, z_count, x_count),
         weight_grad.reshape(27, channels, out_count),

time: 99.8 us -> 98.1 us (0.983)
  other arithmetic: 0 us -> 5.26 us
  local copies, waits for them, and re-layouts: 10.6 us -> 6.41 us
  Pallas kernels: 87.9 us -> 85.5 us
    select_n x0 -> x1, other arithmetic: none -> 4.32 us  [local(): jnp.where(wide < 0, -size, size).reshape(9, 2, line * per, out_count)]
    unnamed x4 -> x3, local copies, waits for them, and re-layouts: 10.6 us -> 6.41 us
    pallas_call x1, Pallas kernels: 87.9 us -> 85.5 us  [local(): pl.pallas_call(functools.partial(grads_kernel, x_count, count, norm), out...]
where the time goes in v3:
time: 98.1 us; the launch traced here: 97.8 us
  Pallas kernels  85.5 us (87%)
  local copies, waits for them, and re-layouts  6.41 us (7%)
  other arithmetic  5.26 us (5%)
    pallas_call x1, Pallas kernels, local(): pl.pallas_call(functools.partial(grads_kernel, x_count, count, norm), out...  85.5 us
    unnamed x3, local copies, waits for them, and re-layouts  6.41 us
    select_n x1, other arithmetic, local(): jnp.where(wide < 0, -size, size).reshape(9, 2, line * per, out_count)  4.32 us

profile of v3, /device:TPU:0, one launch (start us, length us, event | category | flops | bytes accessed | tf_op | source)
XLA Modules:
  0.0 97.8 jit_solution(3911952901606125426)
XLA Ops:
  0.6 2.0 %copy.6 = bf16[16,8,8,256]{3,1,2,0:T(8,128)(2,1)} copy(bf16[16,8,8,256]{3,2,1,0:T(8,128)(2,1)} %bitcast.18) | data formatting | bytes 1048576
  2.6 2.5 %copy.7 = bf16[32,8,8,256]{3,1,2,0:T(8,128)(2,1)} copy(bf16[32,8,8,256]{3,2,1,0:T(8,128)(2,1)} %bitcast.17) | data formatting | bytes 2097152
  5.1 85.5 %grads.1 = (bf16[128,2048]{1,0:T(8,128)(2,1)}, bf16[9,2,4,112,128]{4,3,2,1,0:T(8,128)(2,1)}) custom-call(bf16[128,2048]{1,0:T(8,128)(2,1)} %bitcast.16, bf16[256,2048]{1,0:T(8,128)(2,1)} %bitcast.14, bf16[27,256,128]{2,1,0:T(8,128)(2,1)} %w_ref.1), custom_call_target="tpu_custom_call" | custom-call | tf_op jit(solution)/shard_map/grads/pallas_call | solution.py:294
  90.6 2.0 %copy.8 = bf16[16,8,8,256]{3,2,1,0:T(8,128)(2,1)} copy(bf16[16,8,8,256]{3,1,2,0:T(8,128)(2,1)} %bitcast.20) | data formatting | bytes 1048576
  92.5 0.9 convert_multiply_fusion
  93.5 4.3 %negate_select_fusion = f32[9,2,4,96,128]{4,3,2,1,0:T(8,128)} fusion(f32[9,2,4,128]{3,2,1,0:T(4,128)S(1)} %bitcast.21, bf16[9,2,4,112,128]{4,3,2,1,0:T(8,128)(2,1)} %get-tuple-element.5), kind=kLoop, calls=%fused_computation | loop fusion | flops 6193152 | bytes 5345280 | tf_op jit(solution)/shard_map/jit(_where)/select_n | solution.py:337

commit v4 on v3

--- a/solution.py
+++ b/solution.py
@@ -32,9 +32,11 @@
 def grads_kernel(
     x_count, count, norm, own_ref, in_ref, w_ref, out_ref, wg_ref,
     halo, s_ref, dg, dg_in, part, y_out, y_in, half, zz_out, zz_in, z_out, z_in, done,
+    wide_ref, flat_in,
     halo_s, halo_r, y_s, y_r, z_s, z_r, f_s, f_r, g_s, g_r, c_s, c_r,
 ):
-    out_count, cells = own_ref.shape
+    out_count, z_count, _ = own_ref.shape
+    cells = z_count * x_count
     channels = in_ref.shape[0]
     me = lax.axis_index("gy")
     core = lax.axis_index("ch")
@@ -71,11 +73,11 @@
 
     @pl.when(me == 0)
     def _():
-        halo[1] = jnp.zeros((out_count, cells), halo.dtype)
+        halo[1] = jnp.zeros(own_ref.shape, halo.dtype)
 
     @pl.when(me == count - 1)
     def _():
-        halo[0] = jnp.zeros((out_count, cells), halo.dtype)
+        halo[0] = jnp.zeros(own_ref.shape, halo.dtype)
 
     early = len(zz_out)
     lot = [slice(0, per + 16) if g < early else slice(None) for g in range(9)]
@@ -103,6 +105,11 @@
         for g in range(9)
     ]
 
+    def flatten(value):
+        rows = value.shape[0]
+        wide_ref[:rows] = value.astype(jnp.float32)
+        return jnp.concatenate([wide_ref[:rows, z, :] for z in range(z_count)], axis=1)
+
     def shift(a):
         if a == 0:
             plane = halo[0]
@@ -111,13 +118,13 @@
         else:
             plane = halo[1]
         column = lax.broadcasted_iota(jnp.int32, (out_count, cells), 1) % x_count
-        wide = plane.astype(jnp.float32)
+        wide = flatten(plane)
         left = jnp.where(column == x_count - 1, 0.0, pltpu.roll(wide, cells - 1, 1))
         right = jnp.where(column == 0, 0.0, pltpu.roll(wide, 1, 1))
         edge = jnp.zeros((3 * out_count, x_count), s_ref.dtype)
         s_ref[a, :, :x_count] = edge
         s_ref[a, :, x_count + cells :] = edge
-        for c, moved in enumerate((left, plane, right)):
+        for c, moved in enumerate((left, wide, right)):
             s_ref[a, c * out_count : (c + 1) * out_count, x_count : x_count + cells] = (
                 moved.astype(s_ref.dtype)
             )
@@ -127,7 +134,7 @@
 
     def produce(g):
         grad = lax.dot_general(
-            in_ref[...], window(*GROUPS[g]), (((1,), (1,)), ((), ())),
+            flat_in[...], window(*GROUPS[g]), (((1,), (1,)), ((), ())),
             preferred_element_type=jnp.float32,
         )
         first, second, third = (
@@ -217,6 +224,7 @@
             dg[...] += terms
 
     owned = channels // 2
+    flat_in[...] = flatten(in_ref[...]).astype(flat_in.dtype)
     shift(1)
     for g in range(3):
         produce(g)
@@ -255,7 +263,10 @@
         forward(g + 3)
         collect(g + 6)
     to_core.wait_recv()
-    out_ref[...] = (dg[pl.ds(core * owned, owned), :] + dg_in[...]).astype(out_ref.dtype)
+    final = dg[pl.ds(core * owned, owned), :] + dg_in[...]
+    for z in range(z_count):
+        wide_ref[:owned, z, :] = final[:, z * x_count : (z + 1) * x_count]
+    out_ref[...] = wide_ref[:owned].astype(out_ref.dtype)
     for g in range(6):
         finish(g)
     for g in range(6, 9):
@@ -294,13 +305,13 @@
     input_grad, codes = pl.pallas_call(
         functools.partial(grads_kernel, x_count, count, norm),
         out_shape=(
-            jax.ShapeDtypeStruct((channels // 2, cells), bf16),
+            jax.ShapeDtypeStruct((channels // 2, rows * z_count, x_count), bf16),
             jax.ShapeDtypeStruct((9, 2, line, per + 16, out_count), bf16),
         ),
         in_specs=[pl.BlockSpec(memory_space=pltpu.VMEM)] * 3,
         out_specs=[pl.BlockSpec(memory_space=pltpu.VMEM)] * 2,
         scratch_shapes=[
-            pltpu.VMEM((2, out_count, cells), bf16),
+            pltpu.VMEM((2, out_count, rows * z_count, x_count), bf16),
             pltpu.VMEM((3, 3 * out_count, cells + 2 * x_count), bf16),
             pltpu.VMEM((channels, cells), f32),
             pltpu.VMEM((channels // 2, cells), f32),
@@ -313,6 +324,8 @@
             pltpu.VMEM((6, line - 1, per + 16, out_count), bf16),
             pltpu.VMEM((6, line - 1, per + 16, out_count), bf16),
             pltpu.VMEM((9, 2, line, per + 16, out_count), bf16),
+            pltpu.VMEM((channels, rows * z_count, x_count), f32),
+            pltpu.VMEM((channels, cells), bf16),
             dma((2,)),
             dma((2,)),
             dma((9,)),
@@ -330,7 +343,11 @@
             collective_id=0, has_side_effects=True, vmem_limit_bytes=56 * 2**20
         ),
         name="grads",
-    )(cotangent.reshape(out_count, cells), inputs.reshape(channels, cells), weight)
+    )(
+        cotangent.reshape(out_count, rows * z_count, x_count),
+        inputs.reshape(channels, rows * z_count, x_count),
+        weight,
+    )
     wide = codes[..., :per, :].astype(f32)
     step = codes[..., per : per + 1, :].astype(f32) * (1.0 / SPAN)
     size = (jnp.log(jnp.abs(wide)) + SPAN / 2) * step

time: 98.1 us -> 92.4 us (0.942)
  local copies, waits for them, and re-layouts: 6.41 us -> 0.8 us
    unnamed x3, local copies, waits for them, and re-layouts: 6.41 us -> 0.8 us
where the time goes in v4:
time: 92.4 us; the launch traced here: 92.3 us
  Pallas kernels  85.5 us (93%)
  other arithmetic  5.32 us (6%)
    pallas_call x1, Pallas kernels, local(): pl.pallas_call(functools.partial(grads_kernel, x_count, count, norm), out...  85.5 us
    select_n x1, other arithmetic, local(): jnp.where(wide < 0, -size, size).reshape(9, 2, line * per, out_count)  4.32 us

profile of v4, /device:TPU:0, one launch (start us, length us, event | category | flops | bytes accessed | tf_op | source)
XLA Modules:
  0.0 92.3 jit_solution(14124942725708211134)
XLA Ops:
  0.6 85.5 %grads.1 = (bf16[128,8,256]{2,1,0:T(8,128)(2,1)}, bf16[9,2,4,112,128]{4,3,2,1,0:T(8,128)(2,1)}) custom-call(bf16[128,8,256]{2,1,0:T(8,128)(2,1)} %bitcast.9, bf16[256,8,256]{2,1,0:T(8,128)(2,1)} %bitcast.8, bf16[27,256,128]{2,1,0:T(8,128)(2,1)} %w_ref.1), custom_call_target="tpu_custom_call" | custom-call | tf_op jit(solution)/shard_map/grads/pallas_call | solution.py:305
  86.1 0.0 copy-start
  86.2 1.0 %convert_multiply_fusion = f32[9,2,4,1,128]{4,3,2,1,0:T(1,128)S(1)} fusion(bf16[9,2,4,112,128]{4,3,2,1,0:T(8,128)(2,1)} %get-tuple-element.5), kind=kLoop, calls=%fused_computation.6 | loop fusion | flops 18432 | bytes 55296 | tf_op jit(solution)/shard_map/mul | solution.py:352
  87.2 4.3 %negate_select_fusion = f32[9,2,4,96,128]{4,3,2,1,0:T(8,128)} fusion(f32[9,2,4,128]{3,2,1,0:T(4,128)S(1)} %bitcast.11, bf16[9,2,4,112,128]{4,3,2,1,0:T(8,128)(2,1)} %get-tuple-element.5), kind=kLoop, calls=%fused_computation | loop fusion | flops 6193152 | bytes 5345280 | tf_op jit(solution)/shard_map/jit(_where)/select_n | solution.py:354
  91.5 0.0 copy-done
  91.5 0.8 copy.7
Async XLA Ops:
  86.1 5.3 %copy-start = (bf16[128,8,256]{2,1,0:T(8,128)(2,1)S(1)}, bf16[128,8,256]{2,1,0:T(8,128)(2,1)}, u32[]{:S(2)}) copy-start(bf16[128,8,256]{2,1,0:T(8,128)(2,1)} %get-tuple-element.4) | copy-start | bytes 1572868
